TPU v7x, 32 devices: a whole 2x2x4 slice. The times are simulated.
32 devices in a mesh: row: 8 (over z, x), col: 4 (over y, core).
Axes of the slice: x: 2, y: 2, z: 4, core: 2. Of those that a mesh axis runs over, the one named last changes fastest.
Arguments:
- t_upper: bfloat16 [3, 4096, 4096], P(None, 'row', 'col'), may hold values from -0.03125 to 0.03125
- t_old: bfloat16 [3, 4096, 24576], P(None, 'row', 'col'), may hold values from -0.03125 to 0.03125
- inverses: bfloat16 [3, 4096, 4096], P(None, 'row', 'col'), may hold values from -1 to 1.5, as said below
- forcing: float32 [3, 4096, 128], P(None, 'row'), may hold values from -6 to 6
- x_old: bfloat16 [24576, 128], P('col'), may hold values from -6 to 6
- offsets: float32 [128], replicated, may hold values from -0.5 to 0.5
- starts: int32 [128], replicated, may hold values from 0 to 36864
- column_map: int32 [128], replicated, may hold values from 0 to 127, each once
- z_cols: bfloat16 [49152, 3, 4096], P('row', None, 'col'), may hold values from -0.0546875 to 0.0546875
- acc: float32 [49152, 128], P(('row', 'col')), may hold values from -6 to 6
Outputs:
- solved: float32 [3, 4096, 128], P(None, ('row', 'col'))
- acc_out: float32 [49152, 128], P(('row', 'col'))
Inputs may be any that keep to these rules, and one draw needn't show every extreme that they name: `inverses`: dense matrices with a dominant positive diagonal.
All inputs are finite; a program needn't handle non-finite values.
Results may differ from a plain program's by a relative error of at most 0.0003.
Values may be sent and summed in bfloat16 or wider, within the bound.
A program may use at most 192 MiB of HBM per device.

v0:
```python
import jax
import jax.numpy as jnp
from jax import lax
from jax.sharding import PartitionSpec as P

NEUMANN = 3


def split_pair(values):
    upper = values.astype(jnp.bfloat16)
    lower = (values - lax.optimization_barrier(upper).astype(jnp.float32)).astype(jnp.bfloat16)
    return jnp.concatenate([upper, lower], axis=-1)


def body(t_upper, t_old, inverses, forcing, x_old, offsets, starts, column_map, z_cols, acc):
    n_col = lax.axis_size("col")
    row_idx = lax.axis_index("row")
    col_idx = lax.axis_index("col")
    steps = forcing.shape[0]
    row_block = t_upper.shape[1]
    col_block = t_upper.shape[2]
    width = forcing.shape[2]
    old_cols = x_old.shape[0]
    full_rows = col_block * n_col
    share = row_block // n_col
    pairs = {}
    count = 0
    for first in range(steps):
        for second in range(first + 1, steps):
            pairs[first, second] = count
            count = count + 1

    def fold_pair(product):
        return product[:, :width] + product[:, width:]

    old_rows = steps * full_rows + col_idx * old_cols + jnp.arange(old_cols, dtype=jnp.int32)
    old_live = old_rows[:, None] < starts[None, :]
    old_vals = jnp.where(old_live, x_old, jnp.zeros_like(x_old))
    local_start = row_idx * row_block + col_idx * share

    def reduce_rows(partial_value):
        return lax.psum_scatter(partial_value, "col", scatter_dimension=0, tiled=True)

    def spread_rows(values):
        return lax.all_gather(values, ("row", "col"), axis=0, tiled=True)

    def own_cols(whole):
        return lax.dynamic_slice_in_dim(whole, col_idx * col_block, col_block, 0)

    solved_full = {}
    pieces = {}
    for step in reversed(range(steps)):
        partial_value = -jnp.dot(t_old[step], old_vals, preferred_element_type=jnp.float32)
        for later in range(step + 1, steps):
            partial_value = partial_value - fold_pair(
                jnp.dot(
                    t_upper[pairs[step, later]],
                    own_cols(solved_full[later]),
                    preferred_element_type=jnp.float32,
                )
            )
        rhs = reduce_rows(partial_value) + lax.dynamic_slice_in_dim(
            forcing[step], col_idx * share, share, 0
        )
        gathered = spread_rows(split_pair(rhs))
        term = reduce_rows(
            fold_pair(
                jnp.dot(inverses[step], own_cols(gathered), preferred_element_type=jnp.float32)
            )
        )
        total = term
        for extra in range(1, NEUMANN):
            gathered = spread_rows(split_pair(term))
            term = (
                reduce_rows(
                    fold_pair(
                        jnp.dot(
                            inverses[step], own_cols(gathered), preferred_element_type=jnp.float32
                        )
                    )
                )
                * offsets[None, :]
            )
            total = total + term
        rows = step * full_rows + local_start + jnp.arange(share, dtype=jnp.int32)
        total = jnp.where(rows[:, None] < starts[None, :], total, jnp.zeros_like(total))
        pieces[step] = total
        solved_full[step] = spread_rows(split_pair(total))
    stacked = jnp.concatenate([own_cols(solved_full[step]) for step in range(steps)], axis=0)
    one_hot = (jnp.arange(width, dtype=jnp.int32)[:, None] == column_map[None, :]).astype(
        jnp.bfloat16
    )
    picked_upper = jnp.dot(stacked[:, :width], one_hot, preferred_element_type=jnp.float32).astype(
        jnp.bfloat16
    )
    picked_lower = jnp.dot(stacked[:, width:], one_hot, preferred_element_type=jnp.float32).astype(
        jnp.bfloat16
    )
    picked = jnp.concatenate([picked_upper, picked_lower], axis=1)
    z_rows = z_cols.shape[0]
    z_flat = z_cols.reshape(z_rows, steps * col_block)
    contribution = lax.psum_scatter(
        fold_pair(jnp.dot(z_flat, picked, preferred_element_type=jnp.float32)),
        "col",
        scatter_dimension=0,
        tiled=True,
    )
    solved = jnp.stack([pieces[step] for step in range(steps)])
    return (solved, acc + contribution)


def solution(mesh):
    placed = (
        P(None, "row", "col"),
        P(None, "row", "col"),
        P(None, "row", "col"),
        P(None, "row", None),
        P("col", None),
        P(),
        P(),
        P(),
        P("row", None, "col"),
        P(("row", "col"), None),
    )
    return jax.shard_map(
        body,
        mesh=mesh,
        in_specs=placed,
        out_specs=(P(None, ("row", "col"), None), P(("row", "col"), None)),
        check_vma=False,
    )
```

profile of v0, /device:TPU:0, one launch (start us, length us, event | category | flops | bytes accessed | tf_op | source)
XLA Modules:
  0.0 1046.3 jit_solution(5368107433902717011)
XLA Ops:
  7.2 6.9 fusion.36
  14.4 22.6 %reduce-scatter.14.cloned.1.call-done = f32[128,128]{0,1:T(8,128)} async-done(((f32[512,128]{0,1:T(8,128)}), f32[128,128]{0,1:T(8,128)}) %reduce-scatter.14.cloned.1.call-update) | async-done | bytes 65552 | tf_op jit(solution)/shard_map/reduce_scatter | solution.py:42
  39.5 54.6 %all-gather.13.cloned.1.call-done = bf16[4096,256]{0,1:T(8,128)(2,1)} async-done(((bf16[128,256]{0,1:T(8,128)(2,1)}), bf16[4096,256]{0,1:T(8,128)(2,1)}) %all-gather.13.cloned.1.call-update) | async-done | bytes 2097168 | tf_op jit(solution)/shard_map/all_gather | solution.py:45
  96.8 19.5 %reduce-scatter.16.cloned.1.call-done = f32[128,128]{0,1:T(8,128)} async-done(((f32[512,128]{0,1:T(8,128)}), f32[128,128]{0,1:T(8,128)}) %reduce-scatter.16.cloned.1.call-update) | async-done | bytes 65552 | tf_op jit(solution)/shard_map/reduce_scatter | solution.py:42
  118.7 54.1 %all-gather.15.cloned.1.call-done = bf16[4096,256]{0,1:T(8,128)(2,1)} async-done(((bf16[128,256]{0,1:T(8,128)(2,1)}), bf16[4096,256]{0,1:T(8,128)(2,1)}) %all-gather.15.cloned.1.call-update) | async-done | bytes 2097168 | tf_op jit(solution)/shard_map/all_gather | solution.py:45
  175.5 19.2 %reduce-scatter.18.cloned.1.call-done = f32[128,128]{0,1:T(8,128)} async-done(((f32[512,128]{0,1:T(8,128)}), f32[128,128]{0,1:T(8,128)}) %reduce-scatter.18.cloned.1.call-update) | async-done | bytes 65552 | tf_op jit(solution)/shard_map/reduce_scatter | solution.py:42
  197.3 54.3 %all-gather.17.cloned.1.call-done = bf16[4096,256]{0,1:T(8,128)(2,1)} async-done(((bf16[128,256]{0,1:T(8,128)(2,1)}), bf16[4096,256]{0,1:T(8,128)(2,1)}) %all-gather.17.cloned.1.call-update) | async-done | bytes 2097168 | tf_op jit(solution)/shard_map/all_gather | solution.py:45
  254.3 19.5 %reduce-scatter.20.cloned.1.call-done = f32[128,128]{0,1:T(8,128)} async-done(((f32[512,128]{0,1:T(8,128)}), f32[128,128]{0,1:T(8,128)}) %reduce-scatter.20.cloned.1.call-update) | async-done | bytes 65552 | tf_op jit(solution)/shard_map/reduce_scatter | solution.py:42
  275.5 55.0 %all-gather.19.cloned.1.call-done = bf16[4096,256]{0,1:T(8,128)(2,1)} async-done(((bf16[128,256]{0,1:T(8,128)(2,1)}), bf16[4096,256]{0,1:T(8,128)(2,1)}) %all-gather.19.cloned.1.call-update) | async-done | bytes 2097168 | tf_op jit(solution)/shard_map/all_gather | solution.py:45
  333.2 6.9 fusion.30
  340.3 18.9 %reduce-scatter.22.cloned.1.call-done = f32[128,128]{0,1:T(8,128)} async-done(((f32[512,128]{0,1:T(8,128)}), f32[128,128]{0,1:T(8,128)}) %reduce-scatter.22.cloned.1.call-update) | async-done | bytes 65552 | tf_op jit(solution)/shard_map/reduce_scatter | solution.py:42
  361.7 54.5 %all-gather.21.cloned.1.call-done = bf16[4096,256]{0,1:T(8,128)(2,1)} async-done(((bf16[128,256]{0,1:T(8,128)(2,1)}), bf16[4096,256]{0,1:T(8,128)(2,1)}) %all-gather.21.cloned.1.call-update) | async-done | bytes 2097168 | tf_op jit(solution)/shard_map/all_gather | solution.py:45
  418.9 19.5 %reduce-scatter.24.cloned.1.call-done = f32[128,128]{0,1:T(8,128)} async-done(((f32[512,128]{0,1:T(8,128)}), f32[128,128]{0,1:T(8,128)}) %reduce-scatter.24.cloned.1.call-update) | async-done | bytes 65552 | tf_op jit(solution)/shard_map/reduce_scatter | solution.py:42
  440.8 54.1 %all-gather.23.cloned.1.call-done = bf16[4096,256]{0,1:T(8,128)(2,1)} async-done(((bf16[128,256]{0,1:T(8,128)(2,1)}), bf16[4096,256]{0,1:T(8,128)(2,1)}) %all-gather.23.cloned.1.call-update) | async-done | bytes 2097168 | tf_op jit(solution)/shard_map/all_gather | solution.py:45
  497.6 19.3 %reduce-scatter.26.cloned.1.call-done = f32[128,128]{0,1:T(8,128)} async-done(((f32[512,128]{0,1:T(8,128)}), f32[128,128]{0,1:T(8,128)}) %reduce-scatter.26.cloned.1.call-update) | async-done | bytes 65552 | tf_op jit(solution)/shard_map/reduce_scatter | solution.py:42
  519.5 54.3 %all-gather.25.cloned.1.call-done = bf16[4096,256]{0,1:T(8,128)(2,1)} async-done(((bf16[128,256]{0,1:T(8,128)(2,1)}), bf16[4096,256]{0,1:T(8,128)(2,1)}) %all-gather.25.cloned.1.call-update) | async-done | bytes 2097168 | tf_op jit(solution)/shard_map/all_gather | solution.py:45
  576.5 19.3 %reduce-scatter.28.cloned.1.call-done = f32[128,128]{0,1:T(8,128)} async-done(((f32[512,128]{0,1:T(8,128)}), f32[128,128]{0,1:T(8,128)}) %reduce-scatter.28.cloned.1.call-update) | async-done | bytes 65552 | tf_op jit(solution)/shard_map/reduce_scatter | solution.py:42
  599.2 53.1 %all-gather.27.cloned.1.call-done = bf16[4096,256]{0,1:T(8,128)(2,1)} async-done(((bf16[128,256]{0,1:T(8,128)(2,1)}), bf16[4096,256]{0,1:T(8,128)(2,1)}) %all-gather.27.cloned.1.call-update) | async-done | bytes 2097168 | tf_op jit(solution)/shard_map/all_gather | solution.py:45
  655.2 6.9 fusion.21
  662.3 18.9 %reduce-scatter.30.cloned.1.call-done = f32[128,128]{0,1:T(8,128)} async-done(((f32[512,128]{0,1:T(8,128)}), f32[128,128]{0,1:T(8,128)}) %reduce-scatter.30.cloned.1.call-update) | async-done | bytes 65552 | tf_op jit(solution)/shard_map/reduce_scatter | solution.py:42
  683.6 54.5 %all-gather.29.cloned.1.call-done = bf16[4096,256]{0,1:T(8,128)(2,1)} async-done(((bf16[128,256]{0,1:T(8,128)(2,1)}), bf16[4096,256]{0,1:T(8,128)(2,1)}) %all-gather.29.cloned.1.call-update) | async-done | bytes 2097168 | tf_op jit(solution)/shard_map/all_gather | solution.py:45
  740.8 19.5 %reduce-scatter.32.cloned.1.call-done = f32[128,128]{0,1:T(8,128)} async-done(((f32[512,128]{0,1:T(8,128)}), f32[128,128]{0,1:T(8,128)}) %reduce-scatter.32.cloned.1.call-update) | async-done | bytes 65552 | tf_op jit(solution)/shard_map/reduce_scatter | solution.py:42
  762.7 54.1 %all-gather.31.cloned.1.call-done = bf16[4096,256]{0,1:T(8,128)(2,1)} async-done(((bf16[128,256]{0,1:T(8,128)(2,1)}), bf16[4096,256]{0,1:T(8,128)(2,1)}) %all-gather.31.cloned.1.call-update) | async-done | bytes 2097168 | tf_op jit(solution)/shard_map/all_gather | solution.py:45
  819.5 19.3 %reduce-scatter.34.cloned.1.call-done = f32[128,128]{0,1:T(8,128)} async-done(((f32[512,128]{0,1:T(8,128)}), f32[128,128]{0,1:T(8,128)}) %reduce-scatter.34.cloned.1.call-update) | async-done | bytes 65552 | tf_op jit(solution)/shard_map/reduce_scatter | solution.py:42
  841.5 54.4 %all-gather.33.cloned.1.call-done = bf16[4096,256]{0,1:T(8,128)(2,1)} async-done(((bf16[128,256]{0,1:T(8,128)(2,1)}), bf16[4096,256]{0,1:T(8,128)(2,1)}) %all-gather.33.cloned.1.call-update) | async-done | bytes 2097168 | tf_op jit(solution)/shard_map/all_gather | solution.py:45
  895.9 1.9 convolution_bitcast_fusion.1
  898.6 19.5 %reduce-scatter.36.cloned.1.call-done = f32[128,128]{0,1:T(8,128)} async-done(((f32[512,128]{0,1:T(8,128)}), f32[128,128]{0,1:T(8,128)}) %reduce-scatter.36.cloned.1.call-update) | async-done | bytes 65552 | tf_op jit(solution)/shard_map/reduce_scatter | solution.py:42
  920.0 48.7 %copy.21 = bf16[6144,3,1024]{0,2,1:T(8,128)(2,1)} copy(bf16[6144,3,1024]{2,0,1:T(8,128)(2,1)} %param.18) | data formatting | bytes 75497472 | tf_op args[8]
  968.7 6.0 all-gather.35.cloned.1.call-done
  976.6 18.9 %convolution_bitcast_fusion = f32[6144,256]{0,1:T(8,128)} fusion(bf16[6144,3072]{0,1:T(8,128)(2,1)} %bitcast.121, bf16[3072,128]{1,0:T(8,128)(2,1)S(1)} %convolution_convert_fusion, bf16[3072,128]{1,0:T(8,128)(2,1)S(1)} %convolution_convert_fusion.1), kind=kOutput, calls=%fused_computation | convolution fusion | flops 9666822144 | bytes 45613056 | tf_op jit(solution)/shard_map/dot_general | solution.py:103
  995.5 4.9 slice_add_fusion
  1002.6 34.8 %reduce-scatter.38.cloned.1.call-done = f32[1536,128]{0,1:T(8,128)} async-done(((f32[6144,128]{0,1:T(8,128)}), f32[1536,128]{0,1:T(8,128)}) %reduce-scatter.38.cloned.1.call-update) | async-done | bytes 786448 | tf_op jit(solution)/shard_map/reduce_scatter | solution.py:102
  (150 shorter events, 63.8 us)
Async XLA Ops:
  7.2 29.9 %reduce-scatter.14.cloned.1.call-start = ((), (), s32[]{:S(2)}) async-start(), calls=%async_computation.13 | async-start | bytes 327680 | tf_op jit(solution)/shard_map/reduce_scatter | solution.py:42
  14.2 80.0 %all-gather.13.cloned.1.call-start = ((), (), s32[]{:S(2)}) async-start(), calls=%async_computation.14 | async-start | bytes 2162688 | tf_op jit(solution)/shard_map/all_gather | solution.py:45
  39.4 76.9 %reduce-scatter.16.cloned.1.call-start = ((), (), s32[]{:S(2)}) async-start(), calls=%async_computation.15 | async-start | bytes 327680 | tf_op jit(solution)/shard_map/reduce_scatter | solution.py:42
  39.5 155.2 %copy-start.8 = (f32[128]{0:T(128)S(1)}, f32[128]{0:T(128)}, u32[]{:S(2)}) copy-start(f32[128]{0:T(128)} %param.15) | copy-start | bytes 1540
  96.8 76.1 %all-gather.15.cloned.1.call-start = ((), (), s32[]{:S(2)}) async-start(), calls=%async_computation.16 | async-start | bytes 2162688 | tf_op jit(solution)/shard_map/all_gather | solution.py:45
  118.7 155.1 %copy-start.2 = (f32[128,128]{0,1:T(8,128)S(1)}, f32[128,128]{0,1:T(8,128)}, u32[]{:S(2)}) copy-start(f32[128,128]{0,1:T(8,128)} %reduce-scatter.16.cloned.1.call-done) | copy-start | bytes 196612
  118.7 155.1 %copy-start.9 = (s32[128]{0:T(128)S(1)}, s32[128]{0:T(128)}, u32[]{:S(2)}) copy-start(s32[128]{0:T(128)} %param.16) | copy-start | bytes 1540
  118.7 76.0 %reduce-scatter.18.cloned.1.call-start = ((), (), s32[]{:S(2)}) async-start(), calls=%async_computation.17 | async-start | bytes 327680 | tf_op jit(solution)/shard_map/reduce_scatter | solution.py:42
  175.5 76.1 %all-gather.17.cloned.1.call-start = ((), (), s32[]{:S(2)}) async-start(), calls=%async_computation.18 | async-start | bytes 2162688 | tf_op jit(solution)/shard_map/all_gather | solution.py:45
  194.7 79.1 %copy-start.5 = (f32[128,128]{0,1:T(8,128)S(1)}, f32[128,128]{0,1:T(8,128)}, u32[]{:S(2)}) copy-start(f32[128,128]{0,1:T(8,128)} %reduce-scatter.18.cloned.1.call-done) | copy-start | bytes 196612
  197.3 76.5 %reduce-scatter.20.cloned.1.call-start = ((), (), s32[]{:S(2)}) async-start(), calls=%async_computation.19 | async-start | bytes 327680 | tf_op jit(solution)/shard_map/reduce_scatter | solution.py:42
  254.2 76.2 %all-gather.19.cloned.1.call-start = ((), (), s32[]{:S(2)}) async-start(), calls=%async_computation.20 | async-start | bytes 2162688 | tf_op jit(solution)/shard_map/all_gather | solution.py:45
  275.4 83.8 %reduce-scatter.22.cloned.1.call-start = ((), (), s32[]{:S(2)}) async-start(), calls=%async_computation.21 | async-start | bytes 327680 | tf_op jit(solution)/shard_map/reduce_scatter | solution.py:42
  340.1 76.0 %all-gather.21.cloned.1.call-start = ((), (), s32[]{:S(2)}) async-start(), calls=%async_computation.22 | async-start | bytes 2162688 | tf_op jit(solution)/shard_map/all_gather | solution.py:45
  361.6 76.8 %reduce-scatter.24.cloned.1.call-start = ((), (), s32[]{:S(2)}) async-start(), calls=%async_computation.23 | async-start | bytes 327680 | tf_op jit(solution)/shard_map/reduce_scatter | solution.py:42
  418.8 76.1 %all-gather.23.cloned.1.call-start = ((), (), s32[]{:S(2)}) async-start(), calls=%async_computation.24 | async-start | bytes 2162688 | tf_op jit(solution)/shard_map/all_gather | solution.py:45
  440.7 155.1 %copy-start.3 = (f32[128,128]{0,1:T(8,128)S(1)}, f32[128,128]{0,1:T(8,128)}, u32[]{:S(2)}) copy-start(f32[128,128]{0,1:T(8,128)} %reduce-scatter.24.cloned.1.call-done) | copy-start | bytes 196612
  440.7 76.2 %reduce-scatter.26.cloned.1.call-start = ((), (), s32[]{:S(2)}) async-start(), calls=%async_computation.25 | async-start | bytes 327680 | tf_op jit(solution)/shard_map/reduce_scatter | solution.py:42
  497.5 76.3 %all-gather.25.cloned.1.call-start = ((), (), s32[]{:S(2)}) async-start(), calls=%async_computation.26 | async-start | bytes 2162688 | tf_op jit(solution)/shard_map/all_gather | solution.py:45
  519.5 76.4 %reduce-scatter.28.cloned.1.call-start = ((), (), s32[]{:S(2)}) async-start(), calls=%async_computation.27 | async-start | bytes 327680 | tf_op jit(solution)/shard_map/reduce_scatter | solution.py:42
  576.5 75.9 %all-gather.27.cloned.1.call-start = ((), (), s32[]{:S(2)}) async-start(), calls=%async_computation.28 | async-start | bytes 2162688 | tf_op jit(solution)/shard_map/all_gather | solution.py:45
  597.5 83.7 %reduce-scatter.30.cloned.1.call-start = ((), (), s32[]{:S(2)}) async-start(), calls=%async_computation.29 | async-start | bytes 327680 | tf_op jit(solution)/shard_map/reduce_scatter | solution.py:42
  662.1 76.0 %all-gather.29.cloned.1.call-start = ((), (), s32[]{:S(2)}) async-start(), calls=%async_computation.30 | async-start | bytes 2162688 | tf_op jit(solution)/shard_map/all_gather | solution.py:45
  683.6 76.8 %reduce-scatter.32.cloned.1.call-start = ((), (), s32[]{:S(2)}) async-start(), calls=%async_computation.31 | async-start | bytes 327680 | tf_op jit(solution)/shard_map/reduce_scatter | solution.py:42
  740.8 76.1 %all-gather.31.cloned.1.call-start = ((), (), s32[]{:S(2)}) async-start(), calls=%async_computation.32 | async-start | bytes 2162688 | tf_op jit(solution)/shard_map/all_gather | solution.py:45
  762.7 155.4 %copy-start.4 = (f32[128,128]{0,1:T(8,128)S(1)}, f32[128,128]{0,1:T(8,128)}, u32[]{:S(2)}) copy-start(f32[128,128]{0,1:T(8,128)} %reduce-scatter.32.cloned.1.call-done) | copy-start | bytes 196612
  762.7 76.2 %reduce-scatter.34.cloned.1.call-start = ((), (), s32[]{:S(2)}) async-start(), calls=%async_computation.33 | async-start | bytes 327680 | tf_op jit(solution)/shard_map/reduce_scatter | solution.py:42
  819.5 76.4 %all-gather.33.cloned.1.call-start = ((), (), s32[]{:S(2)}) async-start(), calls=%async_computation.34 | async-start | bytes 2162688 | tf_op jit(solution)/shard_map/all_gather | solution.py:45
  838.8 79.3 %copy-start.7 = (f32[128,128]{0,1:T(8,128)S(1)}, f32[128,128]{0,1:T(8,128)}, u32[]{:S(2)}) copy-start(f32[128,128]{0,1:T(8,128)} %reduce-scatter.34.cloned.1.call-done) | copy-start | bytes 196612
  841.4 76.7 %reduce-scatter.36.cloned.1.call-start = ((), (), s32[]{:S(2)}) async-start(), calls=%async_computation.35 | async-start | bytes 327680 | tf_op jit(solution)/shard_map/reduce_scatter | solution.py:42
  898.6 76.1 %all-gather.35.cloned.1.call-start = ((), (), s32[]{:S(2)}) async-start(), calls=%async_computation.36 | async-start | bytes 2162688 | tf_op jit(solution)/shard_map/all_gather | solution.py:45
  919.7 117.7 %reduce-scatter.38.cloned.1.call-start = ((), (), s32[]{:S(2)}) async-start(), calls=%async_computation.37 | async-start | bytes 3932160 | tf_op jit(solution)/shard_map/reduce_scatter | solution.py:102
  (4 other events, 94.3 us)
Sparse Core Ops, SparseCore 0:
  14.3 22.7 reduce-scatter.13
  40.9 53.2 all-gather.12
  97.3 18.9 reduce-scatter.15
  119.6 53.2 all-gather.14
  175.7 18.9 reduce-scatter.17
  198.4 53.2 all-gather.16
  254.8 18.9 reduce-scatter.19
  277.2 53.2 all-gather.18
  340.3 18.9 reduce-scatter.21
  362.9 53.2 all-gather.20
  419.4 18.9 reduce-scatter.23
  441.6 53.2 all-gather.22
  497.9 18.9 reduce-scatter.25
  520.6 53.2 all-gather.24
  576.8 18.9 reduce-scatter.27
  599.1 53.2 all-gather.26
  662.2 18.9 reduce-scatter.29
  684.9 53.2 all-gather.28
  741.3 18.9 reduce-scatter.31
  763.6 53.2 all-gather.30
  819.9 18.9 reduce-scatter.33
  842.7 53.2 all-gather.32
  899.1 18.9 reduce-scatter.35
  921.4 53.2 all-gather.34
  1000.5 36.8 reduce-scatter.37
where the time goes:
time: 1050 us
  waiting for transfers between devices  873 us (83%)
  matrix products  62.2 us (6%)
  local copies, waits for them, and re-layouts  55.7 us (5%)
  other arithmetic  39.2 us (4%)
  between operations  14.6 us (1%)
    all_gather x12, waiting for transfers between devices, spread_rows(): return lax.all_gather(values, ('row', 'col'), axis=0, tiled=True)  603 us
    reduce_scatter x12, waiting for transfers between devices, reduce_rows(): lax.psum_scatter(partial_value, 'col', scatter_dimension=0, tiled=True)  235 us
    unnamed x26, local copies, waits for them, and re-layouts  52.1 us
    reduce_scatter x1, waiting for transfers between devices, body(): lax.psum_scatter(fold_pair(jnp.dot(z_flat, picked, preferred_element_type...  34.8 us
  transfers between devices with their start and end apart: 25, of which 25 were waited for; matrix products, arithmetic and copies ran while one was open for 5% of the time, Pallas kernels for 0%

commit v1 on v0

v1 whole, which is shorter than its diff:
```python
import functools

import jax
import jax.numpy as jnp
from jax import lax
from jax.experimental import pallas as pl
from jax.experimental.pallas import tpu as pltpu
from jax.sharding import PartitionSpec as P

NEUMANN = 3
MESH = pl.DeviceIdType.MESH


def pair_indices(steps):
    pairs = {}
    for first in range(steps):
        for second in range(first + 1, steps):
            pairs[first, second] = len(pairs)
    return pairs


def chain_kernel(
    n_row, n_col, upper_ref, inv_ref, old_ref, forcing_ref, offsets_ref, starts_ref,
    solved_ref, xs_ref,
    part_out, part_in, pair_out, pair_in,
    part_send, part_recv, pair_send, pair_recv,
):
    row = lax.axis_index("row")
    col = lax.axis_index("col")
    steps, row_block, width = old_ref.shape
    col_block = upper_ref.shape[2]
    share = row_block // n_col
    ratio = col_block // row_block
    pairs = pair_indices(steps)
    owner_col = row // ratio
    has_self = owner_col == col
    place = lax.rem(row, ratio) * row_block + col * share
    place = pl.multiple_of(place, share)

    barrier = pltpu.get_barrier_semaphore()
    for hop in range(1, n_col):
        pl.semaphore_signal(
            barrier, inc=1, device_id={"row": row, "col": lax.rem(col + hop, n_col)}, device_id_type=MESH
        )
    for extra in range(ratio):
        for source in range(n_col):
            source_row = col * ratio + extra

            @pl.when(jnp.logical_or(source_row != row, source != col))
            def _():
                pl.semaphore_signal(
                    barrier, inc=1, device_id={"row": source_row, "col": source}, device_id_type=MESH
                )

    pl.semaphore_wait(barrier, n_col - 1 + n_row - jnp.where(has_self, 1, 0))

    def fold(product):
        return product[:, :width] + product[:, width:]

    def reduce_rows(k, block):
        copies = []
        for hop in range(n_col - 1, 0, -1):
            target = lax.rem(col + hop, n_col)
            part_out[k, hop - 1] = block(target)
            copy = pltpu.make_async_remote_copy(
                src_ref=part_out.at[k, hop - 1],
                dst_ref=part_in.at[k, hop - 1],
                send_sem=part_send.at[k, hop - 1],
                recv_sem=part_recv.at[k, hop - 1],
                device_id={"row": row, "col": target},
                device_id_type=MESH,
            )
            copy.start()
            copies.append((hop, copy))
        value = block(col)
        for hop, copy in copies:
            copy.wait()
            value = value + part_in[k, hop - 1]
        return value

    def start_spread(k, value):
        upper = value.astype(jnp.bfloat16)
        lower = (value - upper.astype(jnp.float32)).astype(jnp.bfloat16)
        pair_out[k, :, :width] = upper
        pair_out[k, :, width:] = lower
        for hop in range(n_row):
            target = lax.rem(row + hop + 1, n_row)

            def send():
                pltpu.make_async_remote_copy(
                    src_ref=pair_out.at[k],
                    dst_ref=pair_in.at[k, pl.ds(place, share)],
                    send_sem=pair_send.at[k],
                    recv_sem=pair_recv.at[k],
                    device_id={"row": target, "col": owner_col},
                    device_id_type=MESH,
                ).start()

            if hop < n_row - 1:
                send()
            else:
                pl.when(jnp.logical_not(has_self))(send)

        @pl.when(has_self)
        def _():
            pair_in[k, pl.ds(place, share), :width] = upper
            pair_in[k, pl.ds(place, share), width:] = lower

    def wait_all(k, sem):
        for mine, rows in ((True, col_block - share), (False, col_block)):

            @pl.when(has_self == mine)
            def _():
                span = pair_in.at[k, pl.ds(0, rows)]
                pltpu.make_async_copy(span, span, sem.at[k]).wait()

    def spread(k, value):
        start_spread(k, value)
        wait_all(k, pair_recv)

    def times(mat_ref, index, k):
        def block(target):
            rows = pl.ds(pl.multiple_of(target * share, share), share)
            return fold(
                jnp.dot(mat_ref[index, rows, :], pair_in[k], preferred_element_type=jnp.float32)
            )

        return block

    offsets = offsets_ref[...]
    starts = starts_ref[...]
    k = 0
    solved_at = {}
    for step in reversed(range(steps)):

        def rhs_block(target):
            rows = pl.ds(pl.multiple_of(target * share, share), share)
            value = -old_ref[step, rows, :]
            for later in range(step + 1, steps):
                value = value - times(upper_ref, pairs[step, later], solved_at[later])(target)
            return value

        mine = pl.ds(pl.multiple_of(col * share, share), share)
        rhs = reduce_rows(k, rhs_block) + forcing_ref[step, mine, :]
        spread(k, rhs)
        k += 1
        total = None
        for term_index in range(NEUMANN):
            term = reduce_rows(k, times(inv_ref, step, k - 1))
            if term_index:
                term = term * offsets
            total = term if total is None else total + term
            if term_index < NEUMANN - 1:
                spread(k, term)
                k += 1
        first = step * (col_block * n_col) + row * row_block + col * share
        rows = first + lax.broadcasted_iota(jnp.int32, (share, width), 0)
        total = jnp.where(rows < starts, total, 0.0)
        solved_ref[step] = total
        spread(k, total)
        solved_at[step] = k
        k += 1
        xs_ref[step] = pair_in[solved_at[step]]
    for slot in range(k):
        wait_all(slot, pair_send)


def chain(n_row, n_col, t_upper, inverses, old_part, forcing, offsets, starts):
    steps, row_block, width = old_part.shape
    col_block = t_upper.shape[2]
    share = row_block // n_col
    rounds = steps * (NEUMANN + 1)
    vmem = pl.BlockSpec(memory_space=pltpu.VMEM)
    return pl.pallas_call(
        functools.partial(chain_kernel, n_row, n_col),
        out_shape=(
            jax.ShapeDtypeStruct((steps, share, width), jnp.float32),
            jax.ShapeDtypeStruct((steps, col_block, 2 * width), jnp.bfloat16),
        ),
        in_specs=[vmem] * 6,
        out_specs=(vmem, vmem),
        scratch_shapes=[
            pltpu.VMEM((rounds, n_col - 1, share, width), jnp.float32),
            pltpu.VMEM((rounds, n_col - 1, share, width), jnp.float32),
            pltpu.VMEM((rounds, share, 2 * width), jnp.bfloat16),
            pltpu.VMEM((rounds, col_block, 2 * width), jnp.bfloat16),
            pltpu.SemaphoreType.DMA((rounds, n_col - 1)),
            pltpu.SemaphoreType.DMA((rounds, n_col - 1)),
            pltpu.SemaphoreType.DMA((rounds,)),
            pltpu.SemaphoreType.DMA((rounds,)),
        ],
        compiler_params=pltpu.CompilerParams(
            collective_id=0, has_side_effects=True, vmem_limit_bytes=48 * 1024 * 1024
        ),
        name="chain",
    )(t_upper, inverses, old_part, forcing, offsets, starts)


def body(t_upper, t_old, inverses, forcing, x_old, offsets, starts, column_map, z_cols, acc):
    n_col = lax.axis_size("col")
    n_row = lax.axis_size("row")
    col_idx = lax.axis_index("col")
    steps, row_block, width = forcing.shape
    col_block = t_upper.shape[2]
    old_cols = x_old.shape[0]
    full_rows = col_block * n_col

    old_rows = steps * full_rows + col_idx * old_cols + jnp.arange(old_cols, dtype=jnp.int32)
    old_live = old_rows[:, None] < starts[None, :]
    old_vals = jnp.where(old_live, x_old, jnp.zeros_like(x_old))
    old_part = jnp.dot(
        t_old.reshape(steps * row_block, old_cols), old_vals, preferred_element_type=jnp.float32
    ).reshape(steps, row_block, width)
    solved, stacked = chain(
        n_row, n_col, t_upper, inverses, old_part, forcing, offsets[None, :], starts[None, :]
    )
    one_hot = (jnp.arange(width, dtype=jnp.int32)[:, None] == column_map[None, :]).astype(
        jnp.bfloat16
    )
    picked = jnp.concatenate(
        [
            jnp.dot(stacked[..., :width], one_hot, preferred_element_type=jnp.float32),
            jnp.dot(stacked[..., width:], one_hot, preferred_element_type=jnp.float32),
        ],
        axis=-1,
    ).astype(jnp.bfloat16)
    by_step = jnp.transpose(z_cols, (1, 0, 2))
    product = sum(
        jnp.dot(by_step[step], picked[step], preferred_element_type=jnp.float32)
        for step in range(steps)
    )
    contribution = lax.psum_scatter(
        product[:, :width] + product[:, width:], "col", scatter_dimension=0, tiled=True
    )
    return (solved, acc + contribution)


def solution(mesh):
    placed = (
        P(None, "row", "col"),
        P(None, "row", "col"),
        P(None, "row", "col"),
        P(None, "row", None),
        P("col", None),
        P(),
        P(),
        P(),
        P("row", None, "col"),
        P(("row", "col"), None),
    )
    return jax.shard_map(
        body,
        mesh=mesh,
        in_specs=placed,
        out_specs=(P(None, ("row", "col"), None), P(("row", "col"), None)),
        check_vma=False,
    )
```

time: 1050 us -> 322 us (0.31)
  waiting for transfers between devices: 873 us -> 43.9 us
  Pallas kernels: 0 us -> 207 us
  local copies, waits for them, and re-layouts: 55.7 us -> 2.37 us
  other arithmetic: 39.2 us -> 6.17 us
  matrix products: 62.2 us -> 48.4 us
    all_gather x12 -> x0, waiting for transfers between devices: 603 us -> none  [spread_rows(): return lax.all_gather(values, ('row', 'col'), axis=0, tiled=True)]
    reduce_scatter x13 -> x1, waiting for transfers between devices: 270 us -> 43.9 us  [body(): lax.psum_scatter(product[:, :width] + product[:, width:], 'col', scatter_...]
    pallas_call x0 -> x1, Pallas kernels: none -> 207 us  [chain(): pl.pallas_call(functools.partial(chain_kernel, n_row, n_col), out_shape=(...]
    unnamed x26 -> x13, local copies, waits for them, and re-layouts: 52.1 us -> 2.12 us
    convert_element_type x24 -> x0, other arithmetic: 18.8 us -> none  [the longest x12 10.9 us: split_pair(): upper = values.astype(jnp.bfloat16)]
    dot_general x18 -> x6, matrix products: 62.2 us -> 48.4 us  [the longest x3 35.7 us: body(): jnp.dot(by_step[step], picked[step], preferred_element_type=jnp.float32)]
  transfers between devices with their start and end apart: 25 -> 1, of which waited for: 25 -> 1; matrix products, arithmetic and copies ran while one was open for 5% -> 0% of each run, Pallas kernels for 0% -> 0%
where the time goes in v1:
time: 322 us
  Pallas kernels  207 us (64%)
  matrix products  48.4 us (15%)
  waiting for transfers between devices  43.9 us (14%)
  between operations  14.2 us (4%)
  other arithmetic  6.17 us (2%)
    pallas_call x1, Pallas kernels, chain(): pl.pallas_call(functools.partial(chain_kernel, n_row, n_col), out_shape=(...  207 us
    reduce_scatter x1, waiting for transfers between devices, body(): lax.psum_scatter(product[:, :width] + product[:, width:], 'col', scatter_...  43.9 us
    dot_general x3, matrix products, body(): jnp.dot(by_step[step], picked[step], preferred_element_type=jnp.float32)  35.7 us
    dot_general x1, matrix products, body(): jnp.dot(t_old.reshape(steps * row_block, old_cols), old_vals, preferred_e...  11.9 us
  transfers between devices with their start and end apart: 1, of which 1 were waited for; matrix products, arithmetic and copies ran while one was open for 0% of the time, Pallas kernels for 0%

profile of v1, /device:TPU:0, one launch (start us, length us, event | category | flops | bytes accessed | tf_op | source)
XLA Modules:
  0.0 322.1 jit_solution(1762903903462132471)
XLA Ops:
  7.2 0.0 reduce-scatter.2.cloned.1.call-start
  7.2 0.0 copy-start
  7.2 0.0 copy-start.1
  7.3 0.0 copy-start.2
  7.3 11.9 %convolution_bitcast_fusion = f32[1536,128]{0,1:T(8,128)S(1)} fusion(bf16[1536,6144]{1,0:T(8,128)(2,1)} %bitcast.44, bf16[6144,128]{1,0:T(8,128)(2,1)} %param.14, s32[128]{0:T(128)} %param.16, s32[6144]{0:T(1024)S(1)} %iota_add_fusion), kind=kOutput, calls=%fused_computation.11 | convolution fusion | flops 2417491968 | bytes 21258752 | tf_op jit(solution)/shard_map/dot_general | solution.py:211
  19.2 0.0 copy-start.4
  19.2 0.3 copy.12
  19.4 0.0 copy-done
  19.5 0.0 copy-done.1
  19.5 0.0 copy-done.2
  19.5 207.0 %chain.1 = (f32[3,128,128]{2,1,0:T(8,128)S(1)}, bf16[3,1024,256]{2,1,0:T(8,128)(2,1)S(1)}) custom-call(bf16[3,512,1024]{2,1,0:T(8,128)(2,1)} %upper_ref.1, bf16[3,512,1024]{2,1,0:T(8,128)(2,1)} %inv_ref.1, f32[3,512,128]{2,1,0:T(8,128)S(1)} %bitcast.38, f32[3,512,128]{2,1,0:T(8,128)S(1)} %copy-done, f32[1,128]{1,0:T(1,128)S(1)} %bitcast.40, ...), custom_call_target="tpu_custom_call" | custom-call | tf_op jit(solution)/shard_map/chain/pallas_call | solution.py:174
  226.5 0.0 copy-done.4
  226.5 0.4 convolution_convert_fusion
  226.9 0.4 convolution_convert_fusion.1
  227.3 10.7 %fusion.1 = f32[256,6144]{1,0:T(8,128)} fusion(bf16[3,6144,1024]{2,1,0:T(8,128)(2,1)} %bitcast.41, bf16[3,1024,128]{1,2,0:T(8,128)(2,1)S(1)} %convolution_convert_fusion.1, bf16[3,1024,128]{1,2,0:T(8,128)(2,1)S(1)} %convolution_convert_fusion), kind=kOutput, calls=%fused_computation.3 | convolution fusion | flops 3222274048 | bytes 20447232 | tf_op jit(solution)/shard_map/dot_general | solution.py:229
  238.0 10.7 %fusion = f32[256,6144]{1,0:T(8,128)} fusion(bf16[3,6144,1024]{2,1,0:T(8,128)(2,1)} %bitcast.42, bf16[3,1024,128]{1,2,0:T(8,128)(2,1)S(1)} %convolution_convert_fusion, bf16[3,1024,128]{1,2,0:T(8,128)(2,1)S(1)} %convolution_convert_fusion.1), kind=kOutput, calls=%fused_computation.1 | convolution fusion | flops 3222274048 | bytes 20447232 | tf_op jit(solution)/shard_map/dot_general | solution.py:229
  248.7 14.3 %fusion.5 = f32[6144,256]{0,1:T(8,128)} fusion(f32[256,6144]{1,0:T(8,128)} %fusion, f32[256,6144]{1,0:T(8,128)} %fusion.1, bf16[3,6144,1024]{2,1,0:T(8,128)(2,1)} %bitcast.43, bf16[3,1024,128]{1,2,0:T(8,128)(2,1)S(1)} %convolution_convert_fusion.1, bf16[3,1024,128]{1,2,0:T(8,128)(2,1)S(1)} %convolution_convert_fusion), kind=kOutput, calls=%fused_computation.8 | convolution fusion | flops 3225419776 | bytes 33030144 | tf_op jit(solution)/shard_map/dot_general | solution.py:229
  263.0 0.0 copy-start.3
  263.0 4.9 %slice_add_fusion = f32[6144,128]{0,1:T(8,128)} fusion(f32[6144,256]{0,1:T(8,128)} %fusion.5), kind=kLoop, calls=%fused_computation.9 | loop fusion | flops 786432 | bytes 9437184 | tf_op jit(solution)/shard_map/add | solution.py:233
  268.0 0.0 reduce-scatter.2.cloned.1.call-update
  268.0 0.0 copy-done.3
  268.0 0.3 copy.13
  268.3 43.9 %reduce-scatter.2.cloned.1.call-done = f32[1536,128]{0,1:T(8,128)} async-done(((f32[6144,128]{0,1:T(8,128)}), f32[1536,128]{0,1:T(8,128)}) %reduce-scatter.2.cloned.1.call-update) | async-done | bytes 786448 | tf_op jit(solution)/shard_map/reduce_scatter | solution.py:232
  312.2 1.2 add.34
  313.4 1.1 copy.14
  314.5 0.7 copy.16
  (1 shorter events, 0.0 us)
Async XLA Ops:
  7.2 305.0 %reduce-scatter.2.cloned.1.call-start = ((), (), s32[]{:S(2)}) async-start(), calls=%async_computation.1 | async-start | bytes 3932160 | tf_op jit(solution)/shard_map/reduce_scatter | solution.py:232
  7.2 12.2 %copy-start = (f32[3,512,128]{2,1,0:T(8,128)S(1)}, f32[3,512,128]{2,1,0:T(8,128)}, u32[]{:S(2)}) copy-start(f32[3,512,128]{2,1,0:T(8,128)} %forcing_ref.1) | copy-start | bytes 2359300
  7.2 12.2 %copy-start.1 = (s32[128]{0:T(128)S(1)}, s32[128]{0:T(128)}, u32[]{:S(2)}) copy-start(s32[128]{0:T(128)} %param.16) | copy-start | bytes 1540
  7.3 12.2 %copy-start.2 = (f32[128]{0:T(128)S(1)}, f32[128]{0:T(128)}, u32[]{:S(2)}) copy-start(f32[128]{0:T(128)} %param.15) | copy-start | bytes 1540
  19.2 207.3 %copy-start.4 = (s32[128]{0:T(128)S(1)}, s32[128]{0:T(128)}, u32[]{:S(2)}) copy-start(s32[128]{0:T(128)} %param.17) | copy-start | bytes 1540
  263.0 5.0 %copy-start.3 = (f32[1536,128]{1,0:T(8,128)S(1)}, f32[1536,128]{1,0:T(8,128)}, u32[]{:S(2)}) copy-start(f32[1536,128]{1,0:T(8,128)} %param.19) | copy-start | bytes 2359300
Sparse Core Ops, SparseCore 0:
  268.1 43.9 reduce-scatter.1

commit v2 on v1

v2 whole, which is shorter than its diff:
```python
import functools
import math

import jax
import jax.numpy as jnp
from jax import lax
from jax.experimental import pallas as pl
from jax.experimental.pallas import tpu as pltpu
from jax.sharding import PartitionSpec as P

NEUMANN = 3
PIECES = 4
OLD_PARTS = 2
MESH = pl.DeviceIdType.MESH


def pair_indices(steps):
    pairs = {}
    for first in range(steps):
        for second in range(first + 1, steps):
            pairs[first, second] = len(pairs)
    return pairs


def chain_kernel(
    n_row, n_col,
    upper_hbm, inv_hbm, old_hbm, z_hbm,
    forcing_ref, x_old_ref, offsets_ref, starts_ref, map_ref, acc_ref,
    solved_ref, acc_out_ref,
    upper_ref, inv_ref, old_buf, z_buf, x_live, old_sum, sel, z_sum,
    part_out, part_in, pair_out, pair_in, core_in, chip_in,
    load_sem, old_sem, z_sem,
    part_send, part_recv, pair_send, pair_recv, pass_send, pass_recv,
    core_send, core_recv, chip_send, chip_recv,
):
    row = lax.axis_index("row")
    col = lax.axis_index("col")
    steps, row_block, width = forcing_ref.shape
    col_block = upper_ref.shape[2]
    share = row_block // n_col
    ratio = col_block // row_block
    old_cols = x_old_ref.shape[0]
    chunk = z_sum.shape[1]
    pairs = pair_indices(steps)
    base_row = row // ratio
    sub_row = lax.rem(row, ratio)
    owner_col = base_row
    has_self = owner_col == col
    groups = n_row // ratio
    place = pl.multiple_of(sub_row * row_block + col * share, share)

    old_cut = old_cols // OLD_PARTS

    def old_copy(index):
        step = steps - 1 - index // OLD_PARTS
        half = index % OLD_PARTS
        slot = index % 2
        return pltpu.make_async_copy(
            old_hbm.at[step, :, pl.ds(half * old_cut, old_cut)], old_buf.at[slot], old_sem.at[slot]
        )

    def z_copy(step, index):
        first = index * chunk
        if not isinstance(index, int):
            first = pl.multiple_of(first, chunk)
        return pltpu.make_async_copy(
            z_hbm.at[step, pl.ds(first, chunk)], z_buf.at[index], z_sem.at[index]
        )

    old_copy(0).start()
    old_copy(1).start()
    inv_copy = pltpu.make_async_copy(inv_hbm, inv_ref, load_sem.at[0])
    upper_copy = pltpu.make_async_copy(upper_hbm, upper_ref, load_sem.at[1])
    inv_copy.start()
    upper_copy.start()
    for index in range(n_col):
        z_copy(steps - 1, index).start()

    barrier = pltpu.get_barrier_semaphore()

    def greet(to_row, to_col):
        pl.semaphore_signal(
            barrier, inc=1, device_id={"row": to_row, "col": to_col}, device_id_type=MESH
        )

    for hop in range(1, n_col):
        greet(row, lax.rem(col + hop, n_col))
    for other in range(1, ratio):
        greet(base_row * ratio + lax.rem(sub_row + other, ratio), col)
    source_row = col * ratio + sub_row
    for hop in range(n_col):
        source = lax.rem(col + hop, n_col)
        if hop:
            greet(source_row, source)
        else:
            pl.when(jnp.logical_not(has_self))(lambda: greet(source_row, source))

    starts = starts_ref[...]
    offsets = offsets_ref[...]
    mask_rows = math.gcd(old_cols, 512)
    old_first = steps * col_block * n_col + col * old_cols

    def mask_tile(tile, carry):
        rows = pl.ds(pl.multiple_of(tile * mask_rows, mask_rows), mask_rows)
        at = old_first + tile * mask_rows + lax.broadcasted_iota(jnp.int32, (mask_rows, width), 0)
        values = x_old_ref[rows, :].astype(jnp.float32)
        x_live[rows, :] = jnp.where(at < starts, values, 0.0).astype(jnp.bfloat16)
        return carry

    lax.fori_loop(0, old_cols // mask_rows, mask_tile, 0)

    def old_work(index):
        step = steps - 1 - index // OLD_PARTS
        half = index % OLD_PARTS
        slot = index % 2
        depth = math.gcd(old_cut, 512)
        old_copy(index).wait()
        if half == 0:
            old_sum[step] = jnp.zeros((row_block, width), jnp.float32)

        def tile_work(tile, carry):
            at = pl.multiple_of(tile * depth, depth)
            old_sum[step] += jnp.dot(
                old_buf[slot, :, pl.ds(at, depth)],
                x_live[pl.ds(half * old_cut + at, depth), :],
                preferred_element_type=jnp.float32,
            )
            return carry

        lax.fori_loop(0, old_cut // depth, tile_work, 0)
        if index + 2 < steps * OLD_PARTS:
            old_copy(index + 2).start()

    def fold(product):
        return product[:, :width] + product[:, width:]

    def select(step, k):
        places = lax.broadcasted_iota(jnp.int32, (width, width), 0)
        one_hot = jnp.where(places == map_ref[...], 1.0, 0.0).astype(jnp.bfloat16)
        for half in range(2):
            lanes = pl.ds(half * width, width)
            sel[step, :, lanes] = jnp.dot(
                pair_in[k, :, lanes], one_hot, preferred_element_type=jnp.float32
            ).astype(jnp.bfloat16)

    def z_work(step, index):
        tall = 512 if chunk % 512 == 0 else chunk
        z_copy(step, index).wait()

        def tile_work(tile, carry):
            rows = pl.ds(pl.multiple_of(tile * tall, tall), tall)
            value = fold(
                jnp.dot(z_buf[index, rows, :], sel[step], preferred_element_type=jnp.float32)
            )
            if step == steps - 1:
                z_sum[index, rows, :] = value
            else:
                z_sum[index, rows, :] += value
            return carry

        lax.fori_loop(0, chunk // tall, tile_work, 0)
        if step:
            z_copy(step - 1, index).start()

    work = {}
    rounds_each = NEUMANN + 1
    left = list(range(OLD_PARTS, steps * OLD_PARTS))
    for number, index in enumerate(left):
        slot = number * rounds_each // len(left)
        work.setdefault(slot, []).append(functools.partial(old_work, index))
    for step in range(steps - 1, 0, -1):
        for index in range(n_col):
            slot = (steps - step) * rounds_each + index * rounds_each // n_col
            work.setdefault(slot, []).append(functools.partial(z_work, step, index))

    def reduce_rows(k, block):
        copies = []
        for hop in range(n_col - 1, 0, -1):
            target = lax.rem(col + hop, n_col)
            part_out[k, hop - 1] = block(target)
            copy = pltpu.make_async_remote_copy(
                src_ref=part_out.at[k, hop - 1],
                dst_ref=part_in.at[k, hop - 1],
                send_sem=part_send.at[k, hop - 1],
                recv_sem=part_recv.at[k, hop - 1],
                device_id={"row": row, "col": target},
                device_id_type=MESH,
            )
            copy.start()
            copies.append((hop, copy))
        value = block(col)
        for hop, copy in copies:
            copy.wait()
            value = value + part_in[k, hop - 1]
        return value

    passed = []

    def spread(k, value):
        upper = value.astype(jnp.bfloat16)
        lower = (value - upper.astype(jnp.float32)).astype(jnp.bfloat16)
        pair_out[k, :, :width] = upper
        pair_out[k, :, width:] = lower
        for hop in range(groups):
            target = lax.rem(base_row + hop + 1, groups) * ratio + sub_row

            def send():
                pltpu.make_async_remote_copy(
                    src_ref=pair_out.at[k],
                    dst_ref=pair_in.at[k, pl.ds(place, share)],
                    send_sem=pair_send.at[k],
                    recv_sem=pair_recv.at[k, col],
                    device_id={"row": target, "col": owner_col},
                    device_id_type=MESH,
                ).start()

            if hop < groups - 1:
                send()
            else:
                pl.when(jnp.logical_not(has_self))(send)

        @pl.when(has_self)
        def _():
            pair_in[k, pl.ds(place, share), :width] = upper
            pair_in[k, pl.ds(place, share), width:] = lower

        for task in work.get(k, ()):
            task()
        arriving = []
        for hop in range(n_col):
            source = lax.rem(col + hop, n_col)
            at = pl.multiple_of(sub_row * row_block + source * share, share)
            span = pair_in.at[k, pl.ds(at, share)]

            def arrived():
                pltpu.make_async_copy(span, span, pair_recv.at[k, source]).wait()

            if hop:
                arrived()
            else:
                pl.when(jnp.logical_not(has_self))(arrived)
            for other in range(1, ratio):
                copy = pltpu.make_async_remote_copy(
                    src_ref=span,
                    dst_ref=span,
                    send_sem=pass_send.at[k, other - 1, hop],
                    recv_sem=pass_recv.at[k, other - 1, hop],
                    device_id={"row": base_row * ratio + lax.rem(sub_row + other, ratio), "col": col},
                    device_id_type=MESH,
                )
                copy.start()
                arriving.append(copy)
        for copy in arriving:
            copy.wait_recv()
        passed.extend(arriving)

    def times(mat_ref, index, k):
        def block(target):
            rows = pl.ds(pl.multiple_of(target * share, share), share)
            return fold(
                jnp.dot(mat_ref[index, rows, :], pair_in[k], preferred_element_type=jnp.float32)
            )

        return block

    for index in range(OLD_PARTS):
        old_work(index)
    pl.semaphore_wait(barrier, n_col - 1 + ratio - 1 + groups - jnp.where(has_self, 1, 0))

    k = 0
    solved_at = {}
    for step in reversed(range(steps)):

        def rhs_block(target):
            rows = pl.ds(pl.multiple_of(target * share, share), share)
            value = -old_sum[step, rows, :]
            for later in range(step + 1, steps):
                value = value - times(upper_ref, pairs[step, later], solved_at[later])(target)
            return value

        mine = pl.ds(pl.multiple_of(col * share, share), share)
        rhs = reduce_rows(k, rhs_block) + forcing_ref[step, mine, :]
        spread(k, rhs)
        k += 1
        if step == steps - 1:
            inv_copy.wait()
            upper_copy.wait()
        total = None
        for term_index in range(NEUMANN):
            term = reduce_rows(k, times(inv_ref, step, k - 1))
            if term_index:
                term = term * offsets
            total = term if total is None else total + term
            if term_index < NEUMANN - 1:
                spread(k, term)
                k += 1
        first = step * (col_block * n_col) + row * row_block + col * share
        rows = first + lax.broadcasted_iota(jnp.int32, (share, width), 0)
        total = jnp.where(rows < starts, total, 0.0)
        solved_ref[step] = total
        spread(k, total)
        solved_at[step] = k
        select(step, k)
        k += 1

    n_pairs = n_col // 2
    half_col = lax.rem(col, 2)
    pair_col = col // 2
    piece = chunk // PIECES
    to_wait = []
    for turn in range(n_pairs):
        target_pair = lax.rem(pair_col + 1 + turn, n_pairs)
        theirs = target_pair * 2 + 1 - half_col
        ours = target_pair * 2 + half_col
        z_work(0, theirs)
        copies = []
        for part in range(PIECES):
            span = pl.ds(part * piece, piece)
            copy = pltpu.make_async_remote_copy(
                src_ref=z_sum.at[theirs, span],
                dst_ref=core_in.at[turn, span],
                send_sem=core_send.at[turn, part],
                recv_sem=core_recv.at[turn, part],
                device_id={"row": row, "col": pair_col * 2 + 1 - half_col},
                device_id_type=MESH,
            )
            copy.start()
            copies.append(copy)
        to_wait.extend(copies)
        z_work(0, ours)
        for part in range(PIECES):
            span = pl.ds(part * piece, piece)
            copies[part].wait_recv()
            if turn == n_pairs - 1:
                acc_out_ref[span, :] = (
                    acc_ref[span, :] + z_sum[ours, span, :] + core_in[turn, span, :]
                )
            else:
                core_in[turn, span, :] += z_sum[ours, span, :]
                copy = pltpu.make_async_remote_copy(
                    src_ref=core_in.at[turn, span],
                    dst_ref=chip_in.at[turn, span],
                    send_sem=chip_send.at[turn, part],
                    recv_sem=chip_recv.at[turn, part],
                    device_id={"row": row, "col": ours},
                    device_id_type=MESH,
                )
                copy.start()
                to_wait.append((copy, turn, span))
    for entry in to_wait:
        if isinstance(entry, tuple):
            copy, turn, span = entry
            copy.wait_recv()
            acc_out_ref[span, :] += chip_in[turn, span, :]
            copy.wait_send()
        else:
            entry.wait_send()
    for copy in passed:
        copy.wait_send()
    for slot in range(k):
        for mine, count in ((True, groups - 1), (False, groups)):

            @pl.when(has_self == mine)
            def _():
                span = pair_in.at[slot, pl.ds(0, count * share)]
                pltpu.make_async_copy(span, span, pair_send.at[slot]).wait()


def chain(n_row, n_col, t_upper, inverses, t_old, by_step, forcing, x_old, offsets, starts, column_map, acc):
    steps, row_block, width = forcing.shape
    col_block = t_upper.shape[2]
    share = row_block // n_col
    ratio = col_block // row_block
    rounds = steps * (NEUMANN + 1)
    old_cols = x_old.shape[0]
    chunk = by_step.shape[1] // n_col
    n_pairs = n_col // 2
    far = max(n_pairs - 1, 1)
    near = max(ratio - 1, 1)
    vmem = pl.BlockSpec(memory_space=pltpu.VMEM)
    hbm = pl.BlockSpec(memory_space=pl.ANY)
    dma = pltpu.SemaphoreType.DMA
    return pl.pallas_call(
        functools.partial(chain_kernel, n_row, n_col),
        out_shape=(
            jax.ShapeDtypeStruct((steps, share, width), jnp.float32),
            jax.ShapeDtypeStruct(acc.shape, jnp.float32),
        ),
        in_specs=[hbm] * 4 + [vmem] * 6,
        out_specs=(vmem, vmem),
        scratch_shapes=[
            pltpu.VMEM(t_upper.shape, jnp.bfloat16),
            pltpu.VMEM(inverses.shape, jnp.bfloat16),
            pltpu.VMEM((2, row_block, old_cols // OLD_PARTS), jnp.bfloat16),
            pltpu.VMEM((n_col, chunk, col_block), jnp.bfloat16),
            pltpu.VMEM((old_cols, width), jnp.bfloat16),
            pltpu.VMEM((steps, row_block, width), jnp.float32),
            pltpu.VMEM((steps, col_block, 2 * width), jnp.bfloat16),
            pltpu.VMEM((n_col, chunk, width), jnp.float32),
            pltpu.VMEM((rounds, n_col - 1, share, width), jnp.float32),
            pltpu.VMEM((rounds, n_col - 1, share, width), jnp.float32),
            pltpu.VMEM((rounds, share, 2 * width), jnp.bfloat16),
            pltpu.VMEM((rounds, col_block, 2 * width), jnp.bfloat16),
            pltpu.VMEM((n_pairs, chunk, width), jnp.float32),
            pltpu.VMEM((far, chunk, width), jnp.float32),
            dma((2,)),
            dma((2,)),
            dma((n_col,)),
            dma((rounds, n_col - 1)),
            dma((rounds, n_col - 1)),
            dma((rounds,)),
            dma((rounds, n_col)),
            dma((rounds, near, n_col)),
            dma((rounds, near, n_col)),
            dma((n_pairs, PIECES)),
            dma((n_pairs, PIECES)),
            dma((far, PIECES)),
            dma((far, PIECES)),
        ],
        compiler_params=pltpu.CompilerParams(
            collective_id=0, has_side_effects=True, vmem_limit_bytes=58 * 1024 * 1024
        ),
        name="chain",
    )(
        t_upper, inverses, t_old, by_step, forcing, x_old,
        offsets[None, :], starts[None, :], column_map[None, :], acc,
    )


def body(t_upper, t_old, inverses, forcing, x_old, offsets, starts, column_map, z_cols, acc):
    n_col = lax.axis_size("col")
    n_row = lax.axis_size("row")
    by_step = jnp.transpose(z_cols, (1, 0, 2))
    return chain(
        n_row, n_col, t_upper, inverses, t_old, by_step, forcing, x_old,
        offsets, starts, column_map, acc,
    )


def solution(mesh):
    placed = (
        P(None, "row", "col"),
        P(None, "row", "col"),
        P(None, "row", "col"),
        P(None, "row", None),
        P("col", None),
        P(),
        P(),
        P(),
        P("row", None, "col"),
        P(("row", "col"), None),
    )
    return jax.shard_map(
        body,
        mesh=mesh,
        in_specs=placed,
        out_specs=(P(None, ("row", "col"), None), P(("row", "col"), None)),
        check_vma=False,
    )
```

time: 322 us -> 245 us (0.76)
  matrix products: 48.4 us -> 0 us
  waiting for transfers between devices: 43.9 us -> 0 us
  Pallas kernels: 207 us -> 240 us
  between operations: 14.2 us -> 0.64 us
  other arithmetic: 6.17 us -> 0 us
    dot_general x6 -> x0, matrix products: 48.4 us -> none  [the longest x3 35.7 us: body(): jnp.dot(by_step[step], picked[step], preferred_element_type=jnp.float32)]
    reduce_scatter x1 -> x0, waiting for transfers between devices: 43.9 us -> none  [body(): lax.psum_scatter(product[:, :width] + product[:, width:], 'col', scatter_...]
    pallas_call x1, Pallas kernels: 207 us -> 240 us  [chain(): pl.pallas_call(functools.partial(chain_kernel, n_row, n_col), out_shape=(...]
    add x3 -> x0, other arithmetic: 6.17 us -> none  [the longest x1 4.95 us: body(): product[:, :width] + product[:, width:]]
  transfers between devices with their start and end apart: 1 -> 0, of which waited for: 1 -> 0; matrix products, arithmetic and copies ran while one was open for 0% -> 0% of each run, Pallas kernels for 0% -> 0%
where the time goes in v2:
time: 245 us; the launch traced here: 244 us
  Pallas kernels  240 us (98%)
  local copies, waits for them, and re-layouts  3.68 us (2%)
    pallas_call x1, Pallas kernels, chain(): pl.pallas_call(functools.partial(chain_kernel, n_row, n_col), out_shape=(...  240 us

profile of v2, /device:TPU:0, one launch (start us, length us, event | category | flops | bytes accessed | tf_op | source)
XLA Modules:
  0.0 244.5 jit_solution(13997599534099817172)
XLA Ops:
  0.6 240.1 %chain.1 = (f32[3,128,128]{2,1,0:T(8,128)}, f32[1536,128]{1,0:T(8,128)}) custom-call(bf16[3,512,1024]{2,1,0:T(8,128)(2,1)} %upper_hbm.1, bf16[3,512,1024]{2,1,0:T(8,128)(2,1)} %inv_hbm.1, bf16[3,512,6144]{2,1,0:T(8,128)(2,1)} %old_hbm.1, bf16[3,6144,1024]{2,1,0:T(8,128)(2,1)} %bitcast.4, f32[3,512,128]{2,1,0:T(8,128)} %forcing_ref.1, ...), custom_call_target="tpu_custom_call" | custom-call | tf_op jit(solution)/shard_map/chain/pallas_call | solution.py:383
  240.8 1.6 copy.14
  242.4 2.1 copy.15

commit v3 on v2

--- a/solution.py
+++ b/solution.py
@@ -25,7 +25,7 @@
 def chain_kernel(
     n_row, n_col,
     upper_hbm, inv_hbm, old_hbm, z_hbm,
-    forcing_ref, x_old_ref, offsets_ref, starts_ref, map_ref, acc_ref,
+    forcing_ref, x_old_ref, offsets_ref, starts_ref, starts_flat, map_ref, acc_ref,
     solved_ref, acc_out_ref,
     upper_ref, inv_ref, old_buf, z_buf, x_live, old_sum, sel, z_sum,
     part_out, part_in, pair_out, pair_in, core_in, chip_in,
@@ -95,8 +95,7 @@
         else:
             pl.when(jnp.logical_not(has_self))(lambda: greet(source_row, source))
 
-    starts = starts_ref[...]
-    offsets = offsets_ref[...]
+    starts = starts_flat[...]
     mask_rows = math.gcd(old_cols, 512)
     old_first = steps * col_block * n_col + col * old_cols
 
@@ -134,14 +133,38 @@
     def fold(product):
         return product[:, :width] + product[:, width:]
 
+    half = width // 2
+    packed_rows = share // 2
+    lanes = lax.broadcasted_iota(jnp.int32, (packed_rows, width), 1)
+    in_front = lanes < half
+
+    def turned(value):
+        return pltpu.roll(value, half, 1)
+
+    def pack(value, side):
+        front, back = value[:packed_rows], value[packed_rows:]
+        if side:
+            return jnp.where(in_front, turned(front), back)
+        return jnp.where(in_front, front, turned(back))
+
+    def pack_product(product):
+        both = product + turned(product)
+        return jnp.where(in_front, both[:packed_rows], both[packed_rows:])
+
     def select(step, k):
-        places = lax.broadcasted_iota(jnp.int32, (width, width), 0)
-        one_hot = jnp.where(places == map_ref[...], 1.0, 0.0).astype(jnp.bfloat16)
-        for half in range(2):
-            lanes = pl.ds(half * width, width)
-            sel[step, :, lanes] = jnp.dot(
-                pair_in[k, :, lanes], one_hot, preferred_element_type=jnp.float32
-            ).astype(jnp.bfloat16)
+        lane = lax.broadcasted_iota(jnp.int32, (width, 2 * width), 0)
+        is_low = lax.broadcasted_iota(jnp.int32, (width, 2 * width), 1) >= width
+        wanted = jnp.concatenate([map_ref[...], map_ref[...]], axis=1)
+        picked = None
+        for side in range(2):
+            column = wanted - side * half
+            inside = jnp.logical_and(column >= 0, column < half)
+            place = jnp.where(is_low, column + half, column)
+            hit = jnp.logical_and(inside, lane == place)
+            one_hot = jnp.where(hit, 1.0, 0.0).astype(jnp.bfloat16)
+            value = jnp.dot(pair_in[2 * k + side], one_hot, preferred_element_type=jnp.float32)
+            picked = value if picked is None else picked + value
+        sel[step] = picked.astype(jnp.bfloat16)
 
     def z_work(step, index):
         tall = 512 if chunk % 512 == 0 else chunk
@@ -171,45 +194,52 @@
     for step in range(steps - 1, 0, -1):
         for index in range(n_col):
             slot = (steps - step) * rounds_each + index * rounds_each // n_col
+            if index == 0:
+                solved_slot = (steps - step) * rounds_each - 1
+                work.setdefault(slot, []).append(functools.partial(select, step, solved_slot))
             work.setdefault(slot, []).append(functools.partial(z_work, step, index))
 
-    def reduce_rows(k, block):
+    def reduce_start(s, block):
         copies = []
         for hop in range(n_col - 1, 0, -1):
             target = lax.rem(col + hop, n_col)
-            part_out[k, hop - 1] = block(target)
+            part_out[s, hop - 1] = block(target)
             copy = pltpu.make_async_remote_copy(
-                src_ref=part_out.at[k, hop - 1],
-                dst_ref=part_in.at[k, hop - 1],
-                send_sem=part_send.at[k, hop - 1],
-                recv_sem=part_recv.at[k, hop - 1],
+                src_ref=part_out.at[s, hop - 1],
+                dst_ref=part_in.at[s, hop - 1],
+                send_sem=part_send.at[s, hop - 1],
+                recv_sem=part_recv.at[s, hop - 1],
                 device_id={"row": row, "col": target},
                 device_id_type=MESH,
             )
             copy.start()
             copies.append((hop, copy))
-        value = block(col)
-        for hop, copy in copies:
-            copy.wait()
-            value = value + part_in[k, hop - 1]
+        return block(col), copies
+
+    def reduce_finish(s, started):
+        value, copies = started
+        for hop, copy in reversed(copies):
+            copy.wait_recv()
+            value = value + part_in[s, hop - 1]
+        to_end.extend(copy for _, copy in copies)
         return value
 
-    passed = []
-
-    def spread(k, value):
-        upper = value.astype(jnp.bfloat16)
-        lower = (value - upper.astype(jnp.float32)).astype(jnp.bfloat16)
-        pair_out[k, :, :width] = upper
-        pair_out[k, :, width:] = lower
+    def spread_start(s, value):
+        upper = value.astype(jnp.bfloat16).astype(jnp.float32)
+        lower = value - upper
+        front = jnp.where(in_front, upper, turned(lower)).astype(jnp.bfloat16)
+        back = jnp.where(in_front, turned(upper), lower).astype(jnp.bfloat16)
+        pair_out[s, :packed_rows] = front
+        pair_out[s, packed_rows:] = back
         for hop in range(groups):
             target = lax.rem(base_row + hop + 1, groups) * ratio + sub_row
 
             def send():
                 pltpu.make_async_remote_copy(
-                    src_ref=pair_out.at[k],
-                    dst_ref=pair_in.at[k, pl.ds(place, share)],
-                    send_sem=pair_send.at[k],
-                    recv_sem=pair_recv.at[k, col],
+                    src_ref=pair_out.at[s],
+                    dst_ref=pair_in.at[s, pl.ds(place, share)],
+                    send_sem=pair_send.at[s],
+                    recv_sem=pair_recv.at[s, col],
                     device_id={"row": target, "col": owner_col},
                     device_id_type=MESH,
                 ).start()
@@ -221,87 +251,121 @@
 
         @pl.when(has_self)
         def _():
-            pair_in[k, pl.ds(place, share), :width] = upper
-            pair_in[k, pl.ds(place, share), width:] = lower
-
-        for task in work.get(k, ()):
-            task()
-        arriving = []
+            pair_in[s, pl.ds(place, share)] = jnp.concatenate([front, back], axis=0)
+
+    def pass_on(s):
         for hop in range(n_col):
             source = lax.rem(col + hop, n_col)
             at = pl.multiple_of(sub_row * row_block + source * share, share)
-            span = pair_in.at[k, pl.ds(at, share)]
+            span = pair_in.at[s, pl.ds(at, share)]
 
             def arrived():
-                pltpu.make_async_copy(span, span, pair_recv.at[k, source]).wait()
+                pltpu.make_async_copy(span, span, pair_recv.at[s, source]).wait()
 
             if hop:
                 arrived()
             else:
                 pl.when(jnp.logical_not(has_self))(arrived)
             for other in range(1, ratio):
-                copy = pltpu.make_async_remote_copy(
+                pltpu.make_async_remote_copy(
                     src_ref=span,
                     dst_ref=span,
-                    send_sem=pass_send.at[k, other - 1, hop],
-                    recv_sem=pass_recv.at[k, other - 1, hop],
+                    send_sem=pass_send.at[s, other - 1],
+                    recv_sem=pass_recv.at[s, other - 1],
                     device_id={"row": base_row * ratio + lax.rem(sub_row + other, ratio), "col": col},
                     device_id_type=MESH,
-                )
-                copy.start()
-                arriving.append(copy)
-        for copy in arriving:
-            copy.wait_recv()
-        passed.extend(arriving)
-
-    def times(mat_ref, index, k):
+                ).start()
+
+    def pass_wait(s, sem, towards):
+        for other in range(1, ratio):
+            source = lax.rem(sub_row + (ratio - other if towards else 0), ratio)
+            at = pl.multiple_of(source * row_block, row_block)
+            span = pair_in.at[s, pl.ds(at, row_block)]
+            pltpu.make_async_copy(span, span, sem.at[s, other - 1]).wait()
+
+    def times(mat_ref, index, s):
         def block(target):
             rows = pl.ds(pl.multiple_of(target * share, share), share)
-            return fold(
-                jnp.dot(mat_ref[index, rows, :], pair_in[k], preferred_element_type=jnp.float32)
+            return pack_product(
+                jnp.dot(mat_ref[index, rows, :], pair_in[s], preferred_element_type=jnp.float32)
             )
 
         return block
+
+    to_end = []
+    totals = {}
+
+    def run(side):
+        offsets = offsets_ref[side]
+        starts = starts_ref[side]
+        solved_at = {}
+        s = side
+        for step in reversed(range(steps)):
+
+            def rhs_block(target):
+                rows = pl.ds(pl.multiple_of(target * share, share), share)
+                value = -pack(old_sum[step, rows, :], side)
+                for later in range(step + 1, steps):
+                    value = value - times(upper_ref, pairs[step, later], solved_at[later])(target)
+                return value
+
+            total = None
+            for phase in range(NEUMANN + 1):
+                if phase == 0:
+                    started = reduce_start(s, rhs_block)
+                else:
+                    started = reduce_start(s, times(inv_ref, step, s - 2))
+                yield
+                value = reduce_finish(s, started)
+                if phase == 0:
+                    mine = pl.ds(pl.multiple_of(col * share, share), share)
+                    value = value + pack(forcing_ref[step, mine, :], side)
+                elif phase > 1:
+                    value = value * offsets
+                if phase:
+                    total = value if total is None else total + value
+                if phase < NEUMANN:
+                    spread_start(s, value)
+                    yield
+                    pass_on(s)
+                    yield
+                    pass_wait(s, pass_recv, True)
+                    s += 2
+            first = step * (col_block * n_col) + row * row_block + col * share
+            rows = first + lax.broadcasted_iota(jnp.int32, (packed_rows, width), 0)
+            rows = rows + jnp.where(in_front, 0, packed_rows)
+            total = jnp.where(rows < starts, total, 0.0)
+            totals[step, side] = total
+            spread_start(s, total)
+            solved_at[step] = s
+            yield
+            pass_on(s)
+            yield
+            pass_wait(s, pass_recv, True)
+            s += 2
 
     for index in range(OLD_PARTS):
         old_work(index)
+    inv_copy.wait()
+    upper_copy.wait()
     pl.semaphore_wait(barrier, n_col - 1 + ratio - 1 + groups - jnp.where(has_self, 1, 0))
 
-    k = 0
-    solved_at = {}
-    for step in reversed(range(steps)):
-
-        def rhs_block(target):
-            rows = pl.ds(pl.multiple_of(target * share, share), share)
-            value = -old_sum[step, rows, :]
-            for later in range(step + 1, steps):
-                value = value - times(upper_ref, pairs[step, later], solved_at[later])(target)
-            return value
-
-        mine = pl.ds(pl.multiple_of(col * share, share), share)
-        rhs = reduce_rows(k, rhs_block) + forcing_ref[step, mine, :]
-        spread(k, rhs)
-        k += 1
-        if step == steps - 1:
-            inv_copy.wait()
-            upper_copy.wait()
-        total = None
-        for term_index in range(NEUMANN):
-            term = reduce_rows(k, times(inv_ref, step, k - 1))
-            if term_index:
-                term = term * offsets
-            total = term if total is None else total + term
-            if term_index < NEUMANN - 1:
-                spread(k, term)
-                k += 1
-        first = step * (col_block * n_col) + row * row_block + col * share
-        rows = first + lax.broadcasted_iota(jnp.int32, (share, width), 0)
-        total = jnp.where(rows < starts, total, 0.0)
-        solved_ref[step] = total
-        spread(k, total)
-        solved_at[step] = k
-        select(step, k)
-        k += 1
+    sides = [run(0), run(1)]
+    for k in range(steps * rounds_each):
+        for stage in range(3):
+            for side in sides:
+                next(side)
+            if stage == 1:
+                for task in work.get(k, ()):
+                    task()
+                if k % rounds_each == NEUMANN:
+                    step = steps - 1 - k // rounds_each
+                    one, two = totals[step, 0], totals[step, 1]
+                    solved_ref[step, :packed_rows] = jnp.where(in_front, one, turned(two))
+                    solved_ref[step, packed_rows:] = jnp.where(in_front, turned(one), two)
+    for side in sides:
+        assert next(side, None) is None
+    select(0, steps * rounds_each - 1)
 
     n_pairs = n_col // 2
     half_col = lax.rem(col, 2)
@@ -355,9 +419,10 @@
             copy.wait_send()
         else:
             entry.wait_send()
-    for copy in passed:
+    for copy in to_end:
         copy.wait_send()
-    for slot in range(k):
+    for slot in range(2 * steps * rounds_each):
+        pass_wait(slot, pass_send, False)
         for mine, count in ((True, groups - 1), (False, groups)):
 
             @pl.when(has_self == mine)
@@ -371,12 +436,17 @@
     col_block = t_upper.shape[2]
     share = row_block // n_col
     ratio = col_block // row_block
-    rounds = steps * (NEUMANN + 1)
+    slots = 2 * steps * (NEUMANN + 1)
     old_cols = x_old.shape[0]
     chunk = by_step.shape[1] // n_col
     n_pairs = n_col // 2
     far = max(n_pairs - 1, 1)
     near = max(ratio - 1, 1)
+
+    def by_side(values):
+        halves = values.reshape(2, 1, width // 2)
+        return jnp.concatenate([halves, halves], axis=2)
+
     vmem = pl.BlockSpec(memory_space=pltpu.VMEM)
     hbm = pl.BlockSpec(memory_space=pl.ANY)
     dma = pltpu.SemaphoreType.DMA
@@ -386,7 +456,7 @@
             jax.ShapeDtypeStruct((steps, share, width), jnp.float32),
             jax.ShapeDtypeStruct(acc.shape, jnp.float32),
         ),
-        in_specs=[hbm] * 4 + [vmem] * 6,
+        in_specs=[hbm] * 4 + [vmem] * 7,
         out_specs=(vmem, vmem),
         scratch_shapes=[
             pltpu.VMEM(t_upper.shape, jnp.bfloat16),
@@ -397,21 +467,21 @@
             pltpu.VMEM((steps, row_block, width), jnp.float32),
             pltpu.VMEM((steps, col_block, 2 * width), jnp.bfloat16),
             pltpu.VMEM((n_col, chunk, width), jnp.float32),
-            pltpu.VMEM((rounds, n_col - 1, share, width), jnp.float32),
-            pltpu.VMEM((rounds, n_col - 1, share, width), jnp.float32),
-            pltpu.VMEM((rounds, share, 2 * width), jnp.bfloat16),
-            pltpu.VMEM((rounds, col_block, 2 * width), jnp.bfloat16),
+            pltpu.VMEM((slots, n_col - 1, share // 2, width), jnp.float32),
+            pltpu.VMEM((slots, n_col - 1, share // 2, width), jnp.float32),
+            pltpu.VMEM((slots, share, width), jnp.bfloat16),
+            pltpu.VMEM((slots, col_block, width), jnp.bfloat16),
             pltpu.VMEM((n_pairs, chunk, width), jnp.float32),
             pltpu.VMEM((far, chunk, width), jnp.float32),
             dma((2,)),
             dma((2,)),
             dma((n_col,)),
-            dma((rounds, n_col - 1)),
-            dma((rounds, n_col - 1)),
-            dma((rounds,)),
-            dma((rounds, n_col)),
-            dma((rounds, near, n_col)),
-            dma((rounds, near, n_col)),
+            dma((slots, n_col - 1)),
+            dma((slots, n_col - 1)),
+            dma((slots,)),
+            dma((slots, n_col)),
+            dma((slots, near)),
+            dma((slots, near)),
             dma((n_pairs, PIECES)),
             dma((n_pairs, PIECES)),
             dma((far, PIECES)),
@@ -423,7 +493,7 @@
         name="chain",
     )(
         t_upper, inverses, t_old, by_step, forcing, x_old,
-        offsets[None, :], starts[None, :], column_map[None, :], acc,
+        by_side(offsets), by_side(starts), starts[None, :], column_map[None, :], acc,
     )
 
 

time: 245 us -> 211 us (0.86)
  Pallas kernels: 240 us -> 204 us
    pallas_call x1, Pallas kernels: 240 us -> 204 us  [chain(): pl.pallas_call(functools.partial(chain_kernel, n_row, n_col), out_shape=(...]
where the time goes in v3:
time: 211 us
  Pallas kernels  204 us (97%)
  local copies, waits for them, and re-layouts  5.15 us (2%)
    pallas_call x1, Pallas kernels, chain(): pl.pallas_call(functools.partial(chain_kernel, n_row, n_col), out_shape=(...  204 us

profile of v3, /device:TPU:0, one launch (start us, length us, event | category | flops | bytes accessed | tf_op | source)
XLA Modules:
  0.0 211.1 jit_solution(4241640493609328254)
XLA Ops:
  0.6 0.7 reshape.10
  1.4 0.6 pad_maximum_fusion.offsets_ref
  2.0 0.7 reshape.11
  2.7 0.6 pad_add_fusion.starts_ref
  3.4 204.0 %chain.1 = (f32[3,128,128]{2,1,0:T(8,128)}, f32[1536,128]{1,0:T(8,128)}) custom-call(bf16[3,512,1024]{2,1,0:T(8,128)(2,1)} %upper_hbm.1, bf16[3,512,1024]{2,1,0:T(8,128)(2,1)} %inv_hbm.1, bf16[3,512,6144]{2,1,0:T(8,128)(2,1)} %old_hbm.1, bf16[3,6144,1024]{2,1,0:T(8,128)(2,1)} %bitcast.5, f32[3,512,128]{2,1,0:T(8,128)} %forcing_ref.1, ...), custom_call_target="tpu_custom_call" | custom-call | tf_op jit(solution)/shard_map/chain/pallas_call | solution.py:453
  207.4 1.6 copy.18
  209.0 2.1 copy.19
